TPU v7x, 256 devices: a whole 4x4x8 slice. The times are simulated.
256 devices in a mesh: row: 16 (over x_lo, z), col: 16 (over x_hi, y, core).
Axes of the slice: x: 4 (x_hi: 2, x_lo: 2; x = x_hi * 2 + x_lo), y: 4, z: 8, core: 2. Of those that a mesh axis runs over, the one named last changes fastest.
Arguments:
- points: bfloat16 [96, 1024, 1024], P('row', 'col')
- targets: bfloat16 [96, 1024, 1000], P('row', 'col'), may hold values from -6 to 6
- coeffs: float32 [96, 1024, 1000], P('row', 'col'), may hold values from -0.25 to 0.25
- block_inverse: float32 [96, 1024, 1024], P('row', 'col')
- block_order: int32 [96], replicated, may hold values from 0 to 95, each once
Outputs:
- coeffs_out: float32 [96, 1024, 1000], P('row', 'col')
All inputs are finite; a program needn't handle non-finite values.
Results may differ from a plain program's by a relative error of at most 0.0003.
Values may be sent and summed in bfloat16 or wider, within the bound.
A program may use at most 64 MiB of HBM per device.

v0:
```python
import jax
import jax.numpy as jnp
from jax import lax
from jax.sharding import PartitionSpec as P

STEPS = 2
ridge_weight = 1.0


def broadcast(value, axis, source):
    kept = jnp.where(lax.axis_index(axis) == source, value, 0).astype(value.dtype)
    return lax.psum(kept, axis)


def on_device(points, targets, coeffs, block_inverse, block_order):
    blocks_here, per_col, features = points.shape
    classes = targets.shape[2]
    my_row = lax.axis_index("row")
    my_col = lax.axis_index("col")
    flat_points = points.reshape(blocks_here * per_col, features)
    flat_wide = flat_points.astype(jnp.float32)
    point_squares = jnp.sum(flat_wide * flat_wide, axis=1)
    current = coeffs
    for sweep_step in range(STEPS):
        block_id = block_order[sweep_step]
        local_index = block_id % blocks_here
        owner_row = block_id // blocks_here
        own_slice = lax.dynamic_index_in_dim(points, local_index, 0, keepdims=False)
        full_block = lax.all_gather(own_slice, "col", axis=0, tiled=True)
        active = broadcast(full_block, "row", owner_row)
        active_wide = active.astype(jnp.float32)
        active_squares = jnp.sum(active_wide * active_wide, axis=1)
        inner = lax.dot_general(
            active, flat_points, (((1,), (1,)), ((), ())), preferred_element_type=jnp.float32
        )
        distance = active_squares[:, None] + point_squares[None, :] - 2.0 * inner
        tile_wide = jnp.exp(-distance * (0.5 / features))
        flat_current = current.reshape(blocks_here * per_col, classes)
        products = jnp.dot(
            tile_wide,
            flat_current,
            precision=lax.Precision.HIGHEST,
            preferred_element_type=jnp.float32,
        )
        summed = lax.psum(products, ("row", "col"))
        own_sum = lax.dynamic_slice_in_dim(summed, my_col * per_col, per_col, 0)
        previous = lax.dynamic_index_in_dim(current, local_index, 0, keepdims=False)
        wanted = lax.dynamic_index_in_dim(targets, local_index, 0, keepdims=False).astype(
            jnp.float32
        )
        residual = wanted - own_sum - ridge_weight * previous
        full_residual = lax.all_gather(residual, "col", axis=0, tiled=True)
        inverse_rows = lax.dynamic_index_in_dim(block_inverse, local_index, 0, keepdims=False)
        increment = jnp.dot(
            inverse_rows,
            full_residual,
            precision=lax.Precision.HIGHEST,
            preferred_element_type=jnp.float32,
        )
        updated = jnp.where(my_row == owner_row, previous + increment, previous)
        current = lax.dynamic_update_index_in_dim(current, updated, local_index, 0)
    return current


def solution(mesh):
    placed = (
        P("row", "col", None),
        P("row", "col", None),
        P("row", "col", None),
        P("row", "col", None),
        P(),
    )
    return jax.shard_map(
        on_device, mesh=mesh, in_specs=placed, out_specs=P("row", "col", None), check_vma=False
    )
```

profile of v0, /device:TPU:1, one launch (start us, length us, event | category | flops | bytes accessed | tf_op | source)
XLA Modules:
  0.0 974.1 jit_solution(10416053570746938592)
XLA Ops:
  6.5 0.0 copy-start
  6.5 0.0 copy-start.5
  6.5 0.0 all-gather.13.cloned.1.call-start
  6.5 1.5 copy.13
  8.1 0.0 copy-done.5
  8.1 0.6 fusion.40
  9.8 1.7 constant_dynamic-slice_fusion.2
  11.5 0.0 all-gather.13.cloned.1.call-update
  11.5 0.0 all-gather.11.cloned.1.call-start
  11.6 0.7 all-gather.11.cloned.1.call-update
  12.3 0.0 all-reduce.9.cloned.1.call-start
  14.6 53.9 %all-gather.13.cloned.1.call-done = bf16[1,1024,1024]{2,1,0:T(8,128)(2,1)} async-done(((bf16[1,64,1024]{2,1,0:T(8,128)(2,1)}), bf16[1,1024,1024]{2,1,0:T(8,128)(2,1)}) %all-gather.13.cloned.1.call-update) | async-done | bytes 2097168 | tf_op jit(solution)/shard_map/all_gather | solution.py:29
  68.5 1.5 select_bitcast_fusion
  69.9 52.7 %all-gather.11.cloned.1.call-done = bf16[1,1024,1024]{2,1,0:T(8,128)(2,1)} async-done(((bf16[1,64,1024]{2,1,0:T(8,128)(2,1)}), bf16[1,1024,1024]{2,1,0:T(8,128)(2,1)}) %all-gather.11.cloned.1.call-update) | async-done | bytes 2097168 | tf_op jit(solution)/shard_map/all_gather | solution.py:29
  122.7 1.4 select_bitcast_fusion.1
  124.1 0.0 all-reduce.9.cloned.1.call-update
  124.1 0.0 all-reduce.5.cloned.1.call-start
  124.2 1.4 multiply_reduce_fusion.2
  125.6 0.1 add.75
  125.6 143.2 %all-reduce.9.cloned.1.call-done = (bf16[1024,1024]{1,0:T(8,128)(2,1)}, bf16[1024,1024]{1,0:T(8,128)(2,1)}) async-done(((bf16[1024,1024]{1,0:T(8,128)(2,1)}, bf16[1024,1024]{1,0:T(8,128)(2,1)}), (bf16[1024,1024]{1,0:T(8,128)(2,1)}, bf16[1024,1024]{1,0:T(8,128)(2,1)})) %all-reduce.9.cloned.1.call-update) | async-done | bytes 4194320 | tf_op jit(solution)/shard_map/psum | solution.py:12
  268.9 2.2 multiply_reduce_fusion.1
  271.1 0.0 copy-done.3
  271.1 2.4 fusion.41
  273.5 8.6 fusion.7
  282.1 0.0 all-reduce.5.cloned.1.call-update
  282.1 0.0 all-gather.7.cloned.1.call-start
  282.2 273.4 %all-reduce.5.cloned.1.call-done = f32[1024,1000]{1,0:T(8,128)} async-done(((f32[1024,1000]{1,0:T(8,128)}), f32[1024,1000]{1,0:T(8,128)}) %all-reduce.5.cloned.1.call-update) | async-done | bytes 4096016 | tf_op jit(solution)/shard_map/psum | solution.py:45
  555.6 1.7 fusion.29
  557.3 0.0 all-gather.7.cloned.1.call-update
  557.3 0.2 all-reduce.7.cloned.1.call-start
  557.5 0.0 copy-start.2
  557.6 2.2 multiply_reduce_fusion
  559.8 0.0 copy-done.2
  559.8 3.6 fusion.42
  563.4 56.2 %all-gather.7.cloned.1.call-done = f32[1024,1000]{1,0:T(8,128)} async-done(((f32[64,1000]{1,0:T(8,128)}), f32[1024,1000]{1,0:T(8,128)}) %all-gather.7.cloned.1.call-update) | async-done | bytes 4096016 | tf_op jit(solution)/shard_map/all_gather | solution.py:52
  619.6 0.0 copy-done
  619.6 4.9 fusion.19
  624.6 0.0 copy-start.1
  624.6 0.0 copy-done.4
  624.6 8.6 fusion
  633.2 0.0 all-reduce.7.cloned.1.call-update
  633.2 0.0 all-gather.9.cloned.1.call-start
  633.3 264.6 %all-reduce.7.cloned.1.call-done = f32[1024,1000]{1,0:T(8,128)} async-done(((f32[1024,1000]{1,0:T(8,128)}), f32[1024,1000]{1,0:T(8,128)}) %all-reduce.7.cloned.1.call-update) | async-done | bytes 4096016 | tf_op jit(solution)/shard_map/psum | solution.py:45
  897.9 1.7 fusion.28
  899.6 0.0 all-gather.9.cloned.1.call-update
  899.6 0.0 copy-done.1
  899.6 62.0 %all-gather.9.cloned.1.call-done = f32[1024,1000]{1,0:T(8,128)} async-done(((f32[64,1000]{1,0:T(8,128)}), f32[1024,1000]{1,0:T(8,128)}) %all-gather.9.cloned.1.call-update) | async-done | bytes 4096016 | tf_op jit(solution)/shard_map/all_gather | solution.py:52
  961.7 5.5 fusion.16
  (4 shorter events, 0.1 us)
Async XLA Ops:
  6.5 613.1 %copy-start = (f32[6,64,1024]{2,1,0:T(8,128)S(1)}, f32[6,64,1024]{2,1,0:T(8,128)}, u32[]{:S(2)}) copy-start(f32[6,64,1024]{2,1,0:T(8,128)} %param.8) | copy-start | bytes 4718596
  6.5 1.5 copy-start.5
  6.5 61.9 %all-gather.13.cloned.1.call-start = ((), (), s32[]{:S(2)}) async-start(), calls=%async_computation.5 | async-start | bytes 2228224 | tf_op jit(solution)/shard_map/all_gather | solution.py:29
  11.5 111.2 %all-gather.11.cloned.1.call-start = ((), (), s32[]{:S(2)}) async-start(), calls=%async_computation.4 | async-start | bytes 2228224 | tf_op jit(solution)/shard_map/all_gather | solution.py:29
  12.3 256.6 %all-reduce.9.cloned.1.call-start = ((), (), s32[]{:S(2)}) async-start(), calls=%async_computation.6 | async-start | bytes 8388608 | tf_op jit(solution)/shard_map/psum | solution.py:12
  124.1 431.4 %all-reduce.5.cloned.1.call-start = ((), (), s32[]{:S(2)}) async-start(), calls=%async_computation | async-start | bytes 8388608 | tf_op jit(solution)/shard_map/psum | solution.py:45
  268.9 2.2 copy-start.3
  282.1 337.5 %all-gather.7.cloned.1.call-start = ((), (), s32[]{:S(2)}) async-start(), calls=%async_computation.1 | async-start | bytes 4456448 | tf_op jit(solution)/shard_map/all_gather | solution.py:52
  557.3 340.5 %all-reduce.7.cloned.1.call-start = ((), (), s32[]{:S(2)}) async-start(), calls=%async_computation.2 | async-start | bytes 8388608 | tf_op jit(solution)/shard_map/psum | solution.py:45
  557.5 2.3 copy-start.2
  619.6 5.0 copy-start.4
  624.6 275.0 %copy-start.1 = (f32[6,64,1000]{2,1,0:T(8,128)}, f32[6,64,1000]{2,1,0:T(8,128)S(1)}, u32[]{:S(2)}) copy-start(f32[6,64,1000]{2,1,0:T(8,128)S(1)} %fusion.19) | copy-start | bytes 4608004
  633.2 328.5 %all-gather.9.cloned.1.call-start = ((), (), s32[]{:S(2)}) async-start(), calls=%async_computation.3 | async-start | bytes 4456448 | tf_op jit(solution)/shard_map/all_gather | solution.py:52
Sparse Core Ops, SparseCore 0:
  11.6 56.7 all-gather.12
  71.2 51.4 all-gather.10
  125.4 143.4 all-reduce.8
  282.3 273.2 all-reduce.4
  558.5 61.0 all-gather.6
  633.3 264.4 all-reduce.6
  900.6 61.0 all-gather.8
where the time goes:
time: 974 us
  waiting for transfers between devices  907 us (93%)
  matrix products  33.7 us (3%)
  between operations  17 us (2%)
  other arithmetic  12.2 us (1%)
    psum x2, waiting for transfers between devices, on_device(): summed = lax.psum(products, ('row', 'col'))  538 us
    psum x1, waiting for transfers between devices, broadcast(): return lax.psum(kept, axis)  143 us
    all_gather x2, waiting for transfers between devices, on_device(): full_residual = lax.all_gather(residual, 'col', axis=0, tiled=True)  118 us
    all_gather x2, waiting for transfers between devices, on_device(): full_block = lax.all_gather(own_slice, 'col', axis=0, tiled=True)  107 us
  transfers between devices with their start and end apart: 7, of which 7 were waited for; matrix products, arithmetic and copies ran while one was open for 1% of the time, Pallas kernels for 0%

commit v1 on v0

--- a/solution.py
+++ b/solution.py
@@ -42,7 +42,7 @@
             precision=lax.Precision.HIGHEST,
             preferred_element_type=jnp.float32,
         )
-        summed = lax.psum(products, ("row", "col"))
+        summed = lax.psum(lax.psum(products, "row"), "col")
         own_sum = lax.dynamic_slice_in_dim(summed, my_col * per_col, per_col, 0)
         previous = lax.dynamic_index_in_dim(current, local_index, 0, keepdims=False)
         wanted = lax.dynamic_index_in_dim(targets, local_index, 0, keepdims=False).astype(

time: 974 us -> 1060 us (1.088)
  waiting for transfers between devices: 907 us -> 992 us
    psum x2 -> x4, waiting for transfers between devices: 538 us -> 621 us  [on_device(): summed = lax.psum(lax.psum(products, 'row'), 'col')]
  transfers between devices with their start and end apart: 7 -> 9, of which waited for: 7 -> 9; matrix products, arithmetic and copies ran while one was open for 1% -> 1% of each run, Pallas kernels for 0% -> 0%
where the time goes in v1:
time: 1060 us
  waiting for transfers between devices  992 us (94%)
  matrix products  33.7 us (3%)
  between operations  16.7 us (2%)
  other arithmetic  12.2 us (1%)
    psum x4, waiting for transfers between devices, on_device(): summed = lax.psum(lax.psum(products, 'row'), 'col')  621 us
    psum x1, waiting for transfers between devices, broadcast(): return lax.psum(kept, axis)  143 us
    all_gather x2, waiting for transfers between devices, on_device(): full_residual = lax.all_gather(residual, 'col', axis=0, tiled=True)  120 us
    all_gather x2, waiting for transfers between devices, on_device(): full_block = lax.all_gather(own_slice, 'col', axis=0, tiled=True)  107 us
  transfers between devices with their start and end apart: 9, of which 9 were waited for; matrix products, arithmetic and copies ran while one was open for 1% of the time, Pallas kernels for 0%

profile of v1, /device:TPU:1, one launch (start us, length us, event | category | flops | bytes accessed | tf_op | source)
XLA Modules:
  0.0 1058.7 jit_solution(6999389776133725543)
XLA Ops:
  6.5 0.0 copy-start
  6.5 0.0 all-gather.13.cloned.1.call-start
  6.5 1.5 copy.15
  8.1 0.6 fusion.40
  9.8 1.7 constant_dynamic-slice_fusion.2
  11.5 0.0 all-gather.13.cloned.1.call-update
  11.5 0.0 all-gather.11.cloned.1.call-start
  11.6 0.7 all-gather.11.cloned.1.call-update
  12.3 0.0 all-reduce.15.cloned.1.call-start
  14.6 53.9 %all-gather.13.cloned.1.call-done = bf16[1,1024,1024]{2,1,0:T(8,128)(2,1)} async-done(((bf16[1,64,1024]{2,1,0:T(8,128)(2,1)}), bf16[1,1024,1024]{2,1,0:T(8,128)(2,1)}) %all-gather.13.cloned.1.call-update) | async-done | bytes 2097168 | tf_op jit(solution)/shard_map/all_gather | solution.py:29
  68.5 1.5 select_bitcast_fusion
  69.9 52.7 %all-gather.11.cloned.1.call-done = bf16[1,1024,1024]{2,1,0:T(8,128)(2,1)} async-done(((bf16[1,64,1024]{2,1,0:T(8,128)(2,1)}), bf16[1,1024,1024]{2,1,0:T(8,128)(2,1)}) %all-gather.11.cloned.1.call-update) | async-done | bytes 2097168 | tf_op jit(solution)/shard_map/all_gather | solution.py:29
  122.7 1.4 select_bitcast_fusion.1
  124.1 0.0 all-reduce.15.cloned.1.call-update
  124.1 0.0 all-reduce.7.cloned.1.call-start
  124.2 1.4 multiply_reduce_fusion.2
  125.6 0.1 add.79
  125.6 143.2 %all-reduce.15.cloned.1.call-done = (bf16[1024,1024]{1,0:T(8,128)(2,1)}, bf16[1024,1024]{1,0:T(8,128)(2,1)}) async-done(((bf16[1024,1024]{1,0:T(8,128)(2,1)}, bf16[1024,1024]{1,0:T(8,128)(2,1)}), (bf16[1024,1024]{1,0:T(8,128)(2,1)}, bf16[1024,1024]{1,0:T(8,128)(2,1)})) %all-reduce.15.cloned.1.call-update) | async-done | bytes 4194320 | tf_op jit(solution)/shard_map/psum | solution.py:12
  268.9 2.2 multiply_reduce_fusion.1
  271.1 2.4 fusion.41
  273.5 8.6 fusion.7
  282.1 0.0 all-reduce.7.cloned.1.call-update
  282.1 0.0 all-reduce.9.cloned.1.call-start
  282.2 151.3 %all-reduce.7.cloned.1.call-done = f32[1024,1000]{1,0:T(8,128)} async-done(((f32[1024,1000]{1,0:T(8,128)}), f32[1024,1000]{1,0:T(8,128)}) %all-reduce.7.cloned.1.call-update) | async-done | bytes 4096016 | tf_op jit(solution)/shard_map/psum | solution.py:45
  433.5 0.0 all-reduce.9.cloned.1.call-update
  433.5 0.0 all-gather.7.cloned.1.call-start
  433.6 163.6 %all-reduce.9.cloned.1.call-done = f32[1024,1000]{1,0:T(8,128)} async-done(((f32[1024,1000]{1,0:T(8,128)}), f32[1024,1000]{1,0:T(8,128)}) %all-reduce.9.cloned.1.call-update) | async-done | bytes 4096016 | tf_op jit(solution)/shard_map/psum | solution.py:45
  597.2 1.7 fusion.29
  598.9 0.0 all-gather.7.cloned.1.call-update
  599.0 0.2 all-reduce.11.cloned.1.call-start
  599.2 2.2 multiply_reduce_fusion
  601.4 0.0 copy-done.2
  601.5 3.6 fusion.42
  605.0 57.0 %all-gather.7.cloned.1.call-done = f32[1024,1000]{1,0:T(8,128)} async-done(((f32[64,1000]{1,0:T(8,128)}), f32[1024,1000]{1,0:T(8,128)}) %all-gather.7.cloned.1.call-update) | async-done | bytes 4096016 | tf_op jit(solution)/shard_map/all_gather | solution.py:52
  662.1 4.9 fusion.19
  667.0 0.0 copy-start.1
  667.0 0.0 copy-done.4
  667.1 8.6 fusion
  675.7 0.0 all-reduce.11.cloned.1.call-update
  675.7 0.0 all-reduce.13.cloned.1.call-start
  675.7 142.1 %all-reduce.11.cloned.1.call-done = f32[1024,1000]{1,0:T(8,128)} async-done(((f32[1024,1000]{1,0:T(8,128)}), f32[1024,1000]{1,0:T(8,128)}) %all-reduce.11.cloned.1.call-update) | async-done | bytes 4096016 | tf_op jit(solution)/shard_map/psum | solution.py:45
  817.8 0.0 all-reduce.13.cloned.1.call-update
  817.8 0.0 all-gather.9.cloned.1.call-start
  817.9 163.8 %all-reduce.13.cloned.1.call-done = f32[1024,1000]{1,0:T(8,128)} async-done(((f32[1024,1000]{1,0:T(8,128)}), f32[1024,1000]{1,0:T(8,128)}) %all-reduce.13.cloned.1.call-update) | async-done | bytes 4096016 | tf_op jit(solution)/shard_map/psum | solution.py:45
  981.6 1.7 fusion.28
  983.4 0.0 all-gather.9.cloned.1.call-update
  983.5 63.2 %all-gather.9.cloned.1.call-done = f32[1024,1000]{1,0:T(8,128)} async-done(((f32[64,1000]{1,0:T(8,128)}), f32[1024,1000]{1,0:T(8,128)}) %all-gather.9.cloned.1.call-update) | async-done | bytes 4096016 | tf_op jit(solution)/shard_map/all_gather | solution.py:52
  1046.7 5.5 fusion.16
  (10 shorter events, 0.1 us)
Async XLA Ops:
  6.5 655.5 %copy-start = (f32[6,64,1024]{2,1,0:T(8,128)S(1)}, f32[6,64,1024]{2,1,0:T(8,128)}, u32[]{:S(2)}) copy-start(f32[6,64,1024]{2,1,0:T(8,128)} %param.8) | copy-start | bytes 4718596
  6.5 1.5 copy-start.5
  6.5 61.9 %all-gather.13.cloned.1.call-start = ((), (), s32[]{:S(2)}) async-start(), calls=%async_computation.7 | async-start | bytes 2228224 | tf_op jit(solution)/shard_map/all_gather | solution.py:29
  11.5 111.2 %all-gather.11.cloned.1.call-start = ((), (), s32[]{:S(2)}) async-start(), calls=%async_computation.6 | async-start | bytes 2228224 | tf_op jit(solution)/shard_map/all_gather | solution.py:29
  12.3 256.6 %all-reduce.15.cloned.1.call-start = ((), (), s32[]{:S(2)}) async-start(), calls=%async_computation.8 | async-start | bytes 8388608 | tf_op jit(solution)/shard_map/psum | solution.py:12
  124.1 309.3 %all-reduce.7.cloned.1.call-start = ((), (), s32[]{:S(2)}) async-start(), calls=%async_computation | async-start | bytes 8388608 | tf_op jit(solution)/shard_map/psum | solution.py:45
  268.9 2.2 copy-start.3
  282.1 315.1 %all-reduce.9.cloned.1.call-start = ((), (), s32[]{:S(2)}) async-start(), calls=%async_computation.1 | async-start | bytes 8388608 | tf_op jit(solution)/shard_map/psum | solution.py:45
  433.5 228.6 %all-gather.7.cloned.1.call-start = ((), (), s32[]{:S(2)}) async-start(), calls=%async_computation.2 | async-start | bytes 4456448 | tf_op jit(solution)/shard_map/all_gather | solution.py:52
  599.0 218.8 %all-reduce.11.cloned.1.call-start = ((), (), s32[]{:S(2)}) async-start(), calls=%async_computation.3 | async-start | bytes 8388608 | tf_op jit(solution)/shard_map/psum | solution.py:45
  599.2 2.3 copy-start.2
  662.1 5.0 copy-start.4
  667.0 316.4 %copy-start.1 = (f32[6,64,1000]{2,1,0:T(8,128)}, f32[6,64,1000]{2,1,0:T(8,128)S(1)}, u32[]{:S(2)}) copy-start(f32[6,64,1000]{2,1,0:T(8,128)S(1)} %fusion.19) | copy-start | bytes 4608004
  675.7 306.0 %all-reduce.13.cloned.1.call-start = ((), (), s32[]{:S(2)}) async-start(), calls=%async_computation.4 | async-start | bytes 8388608 | tf_op jit(solution)/shard_map/psum | solution.py:45
  817.8 228.9 %all-gather.9.cloned.1.call-start = ((), (), s32[]{:S(2)}) async-start(), calls=%async_computation.5 | async-start | bytes 4456448 | tf_op jit(solution)/shard_map/all_gather | solution.py:52
Sparse Core Ops, SparseCore 0:
  11.6 56.7 all-gather.12
  71.2 51.4 all-gather.10
  125.4 143.4 all-reduce.14
  282.3 151.1 all-reduce.6
  436.0 161.1 all-reduce.8
  599.8 62.2 all-gather.6
  675.8 141.9 all-reduce.10
  820.4 161.1 all-reduce.12
  984.4 62.2 all-gather.8

commit v2 on v0

--- a/solution.py
+++ b/solution.py
@@ -9,7 +9,7 @@
 
 def broadcast(value, axis, source):
     kept = jnp.where(lax.axis_index(axis) == source, value, 0).astype(value.dtype)
-    return lax.psum(kept, axis)
+    return jnp.sum(lax.all_gather(kept, axis), axis=0)
 
 
 def on_device(points, targets, coeffs, block_inverse, block_order):

time: 974 us -> 1520 us (1.56)
  waiting for transfers between devices: 907 us -> 1420 us
  other arithmetic: 12.2 us -> 38.4 us
    all_gather x0 -> x2, waiting for transfers between devices: none -> 704 us  [broadcast(): return jnp.sum(lax.all_gather(kept, axis), axis=0)]
    psum x1 -> x0, waiting for transfers between devices: 143 us -> none  [broadcast(): return lax.psum(kept, axis)]
    reduce_sum x0 -> x2, other arithmetic: none -> 26.1 us  [broadcast(): return jnp.sum(lax.all_gather(kept, axis), axis=0)]
    all_gather x2, waiting for transfers between devices: 107 us -> 81.5 us  [on_device(): full_block = lax.all_gather(own_slice, 'col', axis=0, tiled=True)]
  transfers between devices with their start and end apart: 7 -> 8, of which waited for: 7 -> 8; matrix products, arithmetic and copies ran while one was open for 1% -> 3% of each run, Pallas kernels for 0% -> 0%
where the time goes in v2:
time: 1520 us
  waiting for transfers between devices  1420 us (93%)
  other arithmetic  38.4 us (3%)
  matrix products  33.6 us (2%)
  between operations  17.4 us (1%)
    all_gather x2, waiting for transfers between devices, broadcast(): return jnp.sum(lax.all_gather(kept, axis), axis=0)  704 us
    psum x2, waiting for transfers between devices, on_device(): summed = lax.psum(products, ('row', 'col'))  534 us
    all_gather x2, waiting for transfers between devices, on_device(): full_residual = lax.all_gather(residual, 'col', axis=0, tiled=True)  105 us
    all_gather x2, waiting for transfers between devices, on_device(): full_block = lax.all_gather(own_slice, 'col', axis=0, tiled=True)  81.5 us
  transfers between devices with their start and end apart: 8, of which 8 were waited for; matrix products, arithmetic and copies ran while one was open for 3% of the time, Pallas kernels for 0%

profile of v2, /device:TPU:1, one launch (start us, length us, event | category | flops | bytes accessed | tf_op | source)
XLA Modules:
  0.0 1518.6 jit_solution(104090366734618752)
XLA Ops:
  6.5 0.0 copy-start
  6.5 0.0 all-gather.17.cloned.1.call-start
  6.5 1.5 copy.11
  8.1 0.0 copy-done.5
  8.1 0.6 fusion.40
  10.0 1.7 constant_dynamic-slice_fusion.2
  11.6 0.0 all-gather.17.cloned.1.call-update
  11.7 0.0 all-gather.21.cloned.1.call-start
  13.1 55.5 %all-gather.17.cloned.1.call-done = bf16[1,1024,1024]{2,1,0:T(8,128)(2,1)} async-done(((bf16[1,64,1024]{2,1,0:T(8,128)(2,1)}), bf16[1,1024,1024]{2,1,0:T(8,128)(2,1)}) %all-gather.17.cloned.1.call-update) | async-done | bytes 2097168 | tf_op jit(solution)/shard_map/all_gather | solution.py:29
  68.6 1.5 broadcast_select_fusion.1
  70.1 0.0 all-gather.21.cloned.1.call-update
  70.1 0.0 all-gather.19.cloned.1.call-start
  70.2 0.7 all-gather.19.cloned.1.call-update
  70.9 0.0 all-reduce.3.cloned.1.call-start
  70.9 1.4 multiply_reduce_fusion.2
  72.3 0.1 add.71
  72.3 350.3 %all-gather.21.cloned.1.call-done = bf16[1,16384,1024]{2,1,0:T(8,128)(2,1)} async-done(((bf16[1,1024,1024]{2,1,0:T(8,128)(2,1)}), bf16[1,16384,1024]{2,1,0:T(8,128)(2,1)}) %all-gather.21.cloned.1.call-update) | async-done | bytes 33554448 | tf_op jit(solution)/shard_map/all_gather | solution.py:12
  422.6 13.1 reduce_sum.51
  435.7 2.3 multiply_reduce_fusion.1
  438.0 2.4 fusion.41
  440.4 8.6 fusion.7
  449.0 0.0 all-reduce.3.cloned.1.call-update
  449.0 0.0 all-gather.23.cloned.1.call-start
  450.2 26.0 %all-gather.19.cloned.1.call-done = bf16[1,1024,1024]{2,1,0:T(8,128)(2,1)} async-done(((bf16[1,64,1024]{2,1,0:T(8,128)(2,1)}), bf16[1,1024,1024]{2,1,0:T(8,128)(2,1)}) %all-gather.19.cloned.1.call-update) | async-done | bytes 2097168 | tf_op jit(solution)/shard_map/all_gather | solution.py:29
  476.2 1.5 broadcast_select_fusion
  477.6 0.0 all-gather.23.cloned.1.call-update
  477.7 0.0 all-gather.13.cloned.1.call-start
  477.7 269.2 %all-reduce.3.cloned.1.call-done = f32[1024,1000]{1,0:T(8,128)} async-done(((f32[1024,1000]{1,0:T(8,128)}), f32[1024,1000]{1,0:T(8,128)}) %all-reduce.3.cloned.1.call-update) | async-done | bytes 4096016 | tf_op jit(solution)/shard_map/psum | solution.py:45
  746.9 1.7 fusion.29
  748.7 0.0 all-gather.13.cloned.1.call-update
  748.7 0.2 all-reduce.5.cloned.1.call-start
  748.9 353.8 %all-gather.23.cloned.1.call-done = bf16[1,16384,1024]{2,1,0:T(8,128)(2,1)} async-done(((bf16[1,1024,1024]{2,1,0:T(8,128)(2,1)}), bf16[1,16384,1024]{2,1,0:T(8,128)(2,1)}) %all-gather.23.cloned.1.call-update) | async-done | bytes 33554448 | tf_op jit(solution)/shard_map/all_gather | solution.py:12
  1102.8 13.0 reduce_sum.54
  1115.8 2.3 multiply_reduce_fusion
  1118.1 0.1 copy-done.2
  1118.2 3.6 fusion.42
  1121.7 42.5 %all-gather.13.cloned.1.call-done = f32[1024,1000]{1,0:T(8,128)} async-done(((f32[64,1000]{1,0:T(8,128)}), f32[1024,1000]{1,0:T(8,128)}) %all-gather.13.cloned.1.call-update) | async-done | bytes 4096016 | tf_op jit(solution)/shard_map/all_gather | solution.py:52
  1164.3 0.0 copy-done
  1164.3 4.9 fusion.19
  1169.2 0.0 copy-start.1
  1169.3 8.6 fusion
  1177.9 0.0 all-reduce.5.cloned.1.call-update
  1177.9 0.0 all-gather.15.cloned.1.call-start
  1177.9 264.5 %all-reduce.5.cloned.1.call-done = f32[1024,1000]{1,0:T(8,128)} async-done(((f32[1024,1000]{1,0:T(8,128)}), f32[1024,1000]{1,0:T(8,128)}) %all-reduce.5.cloned.1.call-update) | async-done | bytes 4096016 | tf_op jit(solution)/shard_map/psum | solution.py:45
  1442.4 1.7 fusion.28
  1444.1 0.0 all-gather.15.cloned.1.call-update
  1444.2 62.0 %all-gather.15.cloned.1.call-done = f32[1024,1000]{1,0:T(8,128)} async-done(((f32[64,1000]{1,0:T(8,128)}), f32[1024,1000]{1,0:T(8,128)}) %all-gather.15.cloned.1.call-update) | async-done | bytes 4096016 | tf_op jit(solution)/shard_map/all_gather | solution.py:52
  1506.2 5.5 fusion.16
  (9 shorter events, 0.1 us)
Async XLA Ops:
  6.5 1157.7 %copy-start = (f32[6,64,1024]{2,1,0:T(8,128)S(1)}, f32[6,64,1024]{2,1,0:T(8,128)}, u32[]{:S(2)}) copy-start(f32[6,64,1024]{2,1,0:T(8,128)} %param.8) | copy-start | bytes 4718596
  6.5 1.5 copy-start.5
  6.5 62.1 %all-gather.17.cloned.1.call-start = ((), (), s32[]{:S(2)}) async-start(), calls=%async_computation.4 | async-start | bytes 2228224 | tf_op jit(solution)/shard_map/all_gather | solution.py:29
  11.7 411.0 %all-gather.21.cloned.1.call-start = ((), (), s32[]{:S(2)}) async-start(), calls=%async_computation.6 | async-start | bytes 35651584 | tf_op jit(solution)/shard_map/all_gather | solution.py:12
  70.1 406.1 %all-gather.19.cloned.1.call-start = ((), (), s32[]{:S(2)}) async-start(), calls=%async_computation.5 | async-start | bytes 2228224 | tf_op jit(solution)/shard_map/all_gather | solution.py:29
  70.9 676.1 %all-reduce.3.cloned.1.call-start = ((), (), s32[]{:S(2)}) async-start(), calls=%async_computation | async-start | bytes 8388608 | tf_op jit(solution)/shard_map/psum | solution.py:45
  435.7 2.3 copy-start.3
  449.0 653.8 %all-gather.23.cloned.1.call-start = ((), (), s32[]{:S(2)}) async-start(), calls=%async_computation.7 | async-start | bytes 35651584 | tf_op jit(solution)/shard_map/all_gather | solution.py:12
  477.7 686.6 %all-gather.13.cloned.1.call-start = ((), (), s32[]{:S(2)}) async-start(), calls=%async_computation.1 | async-start | bytes 4456448 | tf_op jit(solution)/shard_map/all_gather | solution.py:52
  748.7 693.7 %all-reduce.5.cloned.1.call-start = ((), (), s32[]{:S(2)}) async-start(), calls=%async_computation.2 | async-start | bytes 8388608 | tf_op jit(solution)/shard_map/psum | solution.py:45
  1115.8 2.4 copy-start.2
  1164.3 5.0 copy-start.4
  1169.2 274.9 %copy-start.1 = (f32[6,64,1000]{2,1,0:T(8,128)}, f32[6,64,1000]{2,1,0:T(8,128)S(1)}, u32[]{:S(2)}) copy-start(f32[6,64,1000]{2,1,0:T(8,128)S(1)} %fusion.19) | copy-start | bytes 4608004
  1177.9 328.3 %all-gather.15.cloned.1.call-start = ((), (), s32[]{:S(2)}) async-start(), calls=%async_computation.3 | async-start | bytes 4456448 | tf_op jit(solution)/shard_map/all_gather | solution.py:52
Sparse Core Ops, SparseCore 0:
  11.8 56.7 all-gather.16
  70.4 352.1 all-gather.20
  425.4 50.7 all-gather.18
  481.5 265.3 all-reduce.2
  748.7 354.0 all-gather.22
  1105.8 58.4 all-gather.12
  1178.0 264.3 all-reduce.4
  1445.1 61.0 all-gather.14
